TPU v7x, 512 devices: a whole 4x4x16 slice. The times are simulated.
512 devices in a mesh: tok: 32 (over z, core), wid: 16 (over y, x).
Axes of the slice: x: 4, y: 4, z: 16, core: 2. Of those that a mesh axis runs over, the one named last changes fastest.
Arguments:
- hidden: bfloat16 [16896, 1280], P('tok', 'wid'), may hold values from -30 to 30
- w_qkv: bfloat16 [1280, 1920], P('tok', 'wid'), may hold values from -0.15625 to 0.15625
- w_out: bfloat16 [1280, 1280], P('tok', 'wid'), may hold values from -0.15625 to 0.15625
- w_gate: bfloat16 [1280, 3584], P('tok', 'wid'), may hold values from -0.15625 to 0.15625
- w_up: bfloat16 [1280, 3584], P('tok', 'wid'), may hold values from -0.15625 to 0.15625
- w_down: bfloat16 [3584, 1280], P('wid', 'tok'), may hold values from -0.1875 to 0.1875
- g_attn: float32 [1280], replicated, may hold values from 0.1 to 1.9
- g_ffn: float32 [1280], replicated, may hold values from 0.1 to 1.9
- lengths: int32 [544], P('tok'), may hold values from 0 to 2048, as said below
- k_cache: bfloat16 [544, 2048, 320], P('tok', 'wid'), may hold values from -45 to 45
- v_cache: bfloat16 [544, 2048, 320], P('tok', 'wid'), may hold values from -4 to 4
Outputs:
- output: bfloat16 [16896, 1280], P('tok', 'wid')
- new_kv: bfloat16 [16896, 640], P('tok', 'wid')
Inputs may be any that keep to these rules, and one draw needn't show every extreme that they name: `lengths`: each request's entry is at most 2048, and some request has exactly 2048.
All inputs are finite; a program needn't handle non-finite values.
Results may differ from a plain program's by a relative error of at most 0.017.
Values may be sent and summed in bfloat16 or wider, within the bound.
No kernel may reach another device: no remote copies, remote signals or barrier semaphores. Data moves between devices by JAX's collectives and lax.ppermute only.
A program may use at most 64 MiB of HBM per device.

v0:
```python
import jax
import jax.numpy as jnp
from jax import lax
from jax.sharding import PartitionSpec as P

HEADS = 20
KV_HEADS = 5
HEAD_DIM = 64
STRETCH = 512
EPSILON = 1e-05
MASKED = -1e30
SCORE_SCALE = 0.125


def norm_rows(values, gain):
    wide = values.astype(jnp.float32)
    mean_square = jnp.mean(wide * wide, axis=-1, keepdims=True)
    return (wide * lax.rsqrt(mean_square + EPSILON) * gain).astype(jnp.bfloat16)


def rotate(parts, places):
    half = parts.shape[-1] // 2
    ladder = jnp.arange(half).astype(jnp.float32) * (2.0 / parts.shape[-1])
    freqs = jnp.power(10000.0, -ladder)
    angles = places.astype(jnp.float32)[:, None] * freqs[None, :]
    cosine = jnp.cos(angles)[:, None, :]
    sine = jnp.sin(angles)[:, None, :]
    first = parts[..., :half]
    second = parts[..., half:]
    return jnp.concatenate(
        [first * cosine - second * sine, second * cosine + first * sine], axis=-1
    )


def shards(hidden, w_qkv, w_out, w_gate, w_up, w_down, g_attn, g_ffn, lengths, k_cache, v_cache):
    wid_count = lax.axis_size("wid")
    wid_place = lax.axis_index("wid")
    row_count = hidden.shape[0]
    query_width = HEADS * HEAD_DIM
    kv_width = KV_HEADS * HEAD_DIM
    groups = HEADS // KV_HEADS
    full_rows = lax.all_gather(hidden, "wid", axis=1, tiled=True)
    normed = norm_rows(full_rows, g_attn)
    tall_cols = lax.all_gather(w_qkv, "tok", axis=0, tiled=True)
    own_cols = jnp.dot(normed, tall_cols, preferred_element_type=jnp.float32)
    mixed = lax.all_gather(own_cols.astype(jnp.bfloat16), "wid", axis=1, tiled=True)
    stretch_rows = lengths[0] + jnp.arange(STRETCH)
    places = jnp.concatenate([stretch_rows, lengths[1:]])
    query = rotate(
        mixed[:, :query_width].astype(jnp.float32).reshape(row_count, HEADS, HEAD_DIM), places
    ).astype(jnp.bfloat16)
    keys = rotate(
        mixed[:, query_width : query_width + kv_width]
        .astype(jnp.float32)
        .reshape(row_count, KV_HEADS, HEAD_DIM),
        places,
    ).astype(jnp.bfloat16)
    values = mixed[:, query_width + kv_width :]
    new_kv_all = jnp.concatenate([keys.reshape(row_count, kv_width), values], axis=1)
    kv_share = 2 * kv_width // wid_count
    new_kv = lax.dynamic_slice_in_dim(new_kv_all, wid_place * kv_share, kv_share, 1)
    value_heads = values.reshape(row_count, KV_HEADS, HEAD_DIM)
    span = k_cache.shape[1]
    requests = k_cache.shape[0]
    query_heads = query.reshape(row_count, KV_HEADS, groups, HEAD_DIM)
    old_keys = k_cache.reshape(requests, span, KV_HEADS, HEAD_DIM)
    old_values = v_cache.reshape(requests, span, KV_HEADS, HEAD_DIM)
    spots = wid_place * span + jnp.arange(span)
    live = spots[None, :] < lengths[:, None]
    score_stretch = (
        jnp.einsum(
            "rkgd,pkd->rkgp", query_heads[:STRETCH], old_keys[0], preferred_element_type=jnp.float32
        )
        * SCORE_SCALE
    )
    score_stretch = jnp.where(live[0][None, None, None, :], score_stretch, MASKED)
    score_decode = (
        jnp.einsum(
            "jkgd,jpkd->jkgp",
            query_heads[STRETCH:],
            old_keys[1:],
            preferred_element_type=jnp.float32,
        )
        * SCORE_SCALE
    )
    score_decode = jnp.where(live[1:][:, None, None, :], score_decode, MASKED)
    band = row_count // wid_count
    first_row = wid_place * band
    query_mine = lax.dynamic_slice_in_dim(query_heads, first_row, band, 0)
    later = first_row + jnp.arange(band)[:, None]
    earlier = jnp.arange(row_count)[None, :]
    fresh_ok = (later < STRETCH) & (earlier < STRETCH) & (earlier <= later) | (later >= STRETCH) & (
        earlier == later
    )
    score_fresh = (
        jnp.einsum("rkgd,jkd->rkgj", query_mine, keys, preferred_element_type=jnp.float32)
        * SCORE_SCALE
    )
    score_fresh = jnp.where(fresh_ok[:, None, None, :], score_fresh, MASKED)
    cache_peak = jnp.concatenate([score_stretch.max(-1), score_decode.max(-1)], axis=0)
    fresh_peak = lax.dynamic_update_slice_in_dim(
        jnp.full(cache_peak.shape, MASKED, jnp.float32), score_fresh.max(-1), first_row, 0
    )
    peak = lax.pmax(jnp.maximum(cache_peak, fresh_peak).astype(jnp.bfloat16), "wid").astype(
        jnp.float32
    )
    expo_stretch = jnp.exp(score_stretch - peak[:STRETCH, :, :, None])
    expo_decode = jnp.exp(score_decode - peak[STRETCH:, :, :, None])
    peak_mine = lax.dynamic_slice_in_dim(peak, first_row, band, 0)
    expo_fresh = jnp.exp(score_fresh - peak_mine[:, :, :, None])
    totals = jnp.concatenate([expo_stretch.sum(-1), expo_decode.sum(-1)], axis=0)
    sums = jnp.concatenate(
        [
            jnp.einsum(
                "rkgp,pkd->rkgd",
                expo_stretch.astype(jnp.bfloat16),
                old_values[0],
                preferred_element_type=jnp.float32,
            ),
            jnp.einsum(
                "jkgp,jpkd->jkgd",
                expo_decode.astype(jnp.bfloat16),
                old_values[1:],
                preferred_element_type=jnp.float32,
            ),
        ],
        axis=0,
    )
    fresh_sums = jnp.einsum(
        "rkgj,jkd->rkgd",
        expo_fresh.astype(jnp.bfloat16),
        value_heads,
        preferred_element_type=jnp.float32,
    )
    sums = lax.dynamic_update_slice_in_dim(
        sums, lax.dynamic_slice_in_dim(sums, first_row, band, 0) + fresh_sums, first_row, 0
    )
    totals = lax.dynamic_update_slice_in_dim(
        totals,
        lax.dynamic_slice_in_dim(totals, first_row, band, 0) + expo_fresh.sum(-1),
        first_row,
        0,
    )
    sums_all, totals_all = (
        lax.psum(sums.reshape(row_count, query_width).astype(jnp.bfloat16), "wid").astype(
            jnp.float32
        ),
        lax.psum(totals.reshape(row_count, HEADS).astype(jnp.bfloat16), "wid").astype(jnp.float32),
    )
    merged = sums_all.reshape(row_count, HEADS, HEAD_DIM) / totals_all[:, :, None]
    attended = merged.astype(jnp.bfloat16).reshape(row_count, query_width)
    out_whole = lax.all_gather(w_out, "tok", axis=0, tiled=True)
    projected = jnp.dot(attended, out_whole, preferred_element_type=jnp.float32)
    residual = hidden.astype(jnp.float32) + projected
    middle = residual.astype(jnp.bfloat16)
    middle_full = lax.all_gather(middle, "wid", axis=1, tiled=True)
    normed_ffn = norm_rows(middle_full, g_ffn)
    gate_whole, up_whole = (
        lax.all_gather(w_gate, "tok", axis=0, tiled=True),
        lax.all_gather(w_up, "tok", axis=0, tiled=True),
    )
    gate = jnp.dot(normed_ffn, gate_whole, preferred_element_type=jnp.float32)
    up = jnp.dot(normed_ffn, up_whole, preferred_element_type=jnp.float32)
    activated = (jax.nn.silu(gate) * up).astype(jnp.bfloat16)
    down_full = lax.all_gather(w_down, "tok", axis=1, tiled=True)
    own_sums = lax.psum_scatter(
        lax.dot_general(
            down_full, activated, (((0,), (1,)), ((), ())), preferred_element_type=jnp.float32
        ).astype(jnp.bfloat16),
        "wid",
        scatter_dimension=0,
        tiled=True,
    ).astype(jnp.float32)
    output = (residual + own_sums.T).astype(jnp.bfloat16)
    return (output, new_kv)


def solution(mesh):
    placed = (
        P("tok", "wid"),
        P("tok", "wid"),
        P("tok", "wid"),
        P("tok", "wid"),
        P("tok", "wid"),
        P("wid", "tok"),
        P(),
        P(),
        P("tok"),
        P("tok", "wid", None),
        P("tok", "wid", None),
    )
    return jax.shard_map(
        shards,
        mesh=mesh,
        in_specs=placed,
        out_specs=(P("tok", "wid"), P("tok", "wid")),
        check_vma=False,
    )
```

profile of v0, /device:TPU:2, one launch (start us, length us, event | category | flops | bytes accessed | tf_op | source)
XLA Modules:
  0.0 582.2 jit_solution(18248502710288355273)
XLA Ops:
  7.2 0.7 all-gather.5.cloned.1.call-update
  8.0 37.4 %all_gather.25 = bf16[1280,120]{1,0:T(8,128)(2,1)S(1)} all-gather(bf16[40,120]{1,0:T(8,128)(2,1)} %param.12), channel_id=1, replica_groups=mesh['tok'=32,'wid'=16] {'tok'}, dimensions={0}, use_global_device_ids=true | all-gather | bytes 316800 | tf_op jit(solution)/shard_map/all_gather | solution.py:44
  45.3 29.2 %all-gather.5.cloned.1.call-done = bf16[528,1280]{0,1:T(8,128)(2,1)} async-done(((bf16[528,80]{0,1:T(8,128)(2,1)}), bf16[528,1280]{0,1:T(8,128)(2,1)}) %all-gather.5.cloned.1.call-update) | async-done | bytes 1351696 | tf_op jit(solution)/shard_map/all_gather | solution.py:42
  74.5 1.8 fusion.3
  76.4 3.0 fusion.33
  79.4 1.3 copy-done.5
  80.7 0.6 slice.89
  81.3 1.2 slice.91
  83.8 55.9 %all-gather.9.cloned.1.call-done = bf16[16,120,528]{1,2,0:T(8,128)(2,1)} async-done(((bf16[1,120,528]{1,2,0:T(8,128)(2,1)}), bf16[16,120,528]{1,2,0:T(8,128)(2,1)}) %all-gather.9.cloned.1.call-update) | async-done | bytes 2027536 | tf_op jit(solution)/shard_map/all_gather | solution.py:46
  139.7 2.2 copy.52
  141.8 3.6 reshape.238
  145.4 1.5 slice_convert_fusion
  147.0 2.5 fusion.70
  149.4 2.4 copy.53
  151.8 2.4 subtract_convert_fusion
  154.2 2.7 copy.58
  156.8 2.6 copy.59
  159.5 1.2 fusion.26
  160.8 1.6 copy.57
  162.3 0.9 multiply_subtract_fusion
  163.4 1.1 fusion.72
  164.6 2.0 fusion.71
  166.7 0.9 dynamic_update_slice.9
  167.6 3.3 bitcast_reduce_fusion
  170.9 67.5 %pmax.7 = bf16[528,5,4]{0,2,1:T(4,128)(2,1)S(1)} all-reduce(bf16[528,5,4]{0,2,1:T(4,128)(2,1)S(1)} %fusion.62), channel_id=1, replica_groups=mesh['tok'=32,'wid'=16] {'wid'}, use_global_device_ids=true, to_apply=%region_4.5 | all-reduce | flops 10560 | bytes 42240 | tf_op jit(solution)/shard_map/pmax | solution.py:104
  239.2 0.6 copy-done.9
  239.9 2.2 fusion.59
  242.6 3.9 fusion.19
  246.5 1.5 pad_maximum_fusion
  248.0 1.9 fusion.27
  249.9 6.7 %dynamic_update_slice.10 = bf16[528,5,4,64]{0,3,2,1:T(8,128)(2,1)} dynamic-update-slice(bf16[528,5,4,64]{0,3,2,1:T(8,128)(2,1)} %pad_maximum_fusion, bf16[33,5,4,64]{0,3,2,1:T(8,128)(2,1)} %fusion.27, s32[]{:T(128)S(6)} %select_n.30, s32[]{:T(128)} %constant.11.clone.1, s32[]{:T(128)} %constant.11.clone.1, s32[]{:T(128)} %constant.11.clone.1) | dynamic-update-slice | bytes 168964 | tf_op jit(solution)/shard_map/dynamic_update_slice | solution.py:135
  256.7 31.9 %all_gather.27 = bf16[1280,80]{1,0:T(8,128)(2,1)S(1)} all-gather(bf16[40,80]{1,0:T(8,128)(2,1)S(1)} %copy-done.14), channel_id=1, replica_groups=mesh['tok'=32,'wid'=16] {'tok'}, dimensions={0}, use_global_device_ids=true | all-gather | bytes 211200 | tf_op jit(solution)/shard_map/all_gather | solution.py:152
  289.0 3.7 fusion.1
  293.4 0.9 dynamic_update_slice.11
  294.3 69.2 %psum.15 = bf16[528,20]{0,1:T(8,128)(2,1)S(1)} all-reduce(bf16[528,20]{0,1:T(8,128)(2,1)S(1)} %convert_element_type.114), channel_id=1, replica_groups=mesh['tok'=32,'wid'=16] {'wid'}, use_global_device_ids=true, to_apply=%region_9.10 | all-reduce | flops 10560 | bytes 42240 | tf_op jit(solution)/shard_map/psum | solution.py:148
  363.5 12.9 %all-reduce.3.cloned.1.call-done = bf16[528,1280]{0,1:T(8,128)(2,1)} async-done(((bf16[528,1280]{0,1:T(8,128)(2,1)}), bf16[528,1280]{0,1:T(8,128)(2,1)}) %all-reduce.3.cloned.1.call-update) | async-done | bytes 1351696 | tf_op jit(solution)/shard_map/psum | solution.py:145
  376.3 1.8 fusion.9
  378.1 1.1 fusion.73
  379.3 35.5 %all_gather.29 = bf16[1280,224]{1,0:T(8,128)(2,1)} all-gather(bf16[40,224]{1,0:T(8,128)(2,1)S(1)} %copy-done.11), channel_id=1, replica_groups=mesh['tok'=32,'wid'=16] {'tok'}, dimensions={0}, use_global_device_ids=true | all-gather | bytes 591360 | tf_op jit(solution)/shard_map/all_gather | solution.py:159
  414.8 29.9 %all_gather.30 = bf16[1280,224]{1,0:T(8,128)(2,1)S(1)} all-gather(bf16[40,224]{1,0:T(8,128)(2,1)S(1)} %copy-done.12), channel_id=1, replica_groups=mesh['tok'=32,'wid'=16] {'tok'}, dimensions={0}, use_global_device_ids=true | all-gather | bytes 591360 | tf_op jit(solution)/shard_map/all_gather | solution.py:160
  444.6 33.2 %all_gather.31 = bf16[224,1280]{0,1:T(8,128)(2,1)} all-gather(bf16[224,40]{0,1:T(8,128)(2,1)S(1)} %copy-done.13), channel_id=1, replica_groups=mesh['tok'=32,'wid'=16] {'tok'}, dimensions={1}, use_global_device_ids=true | all-gather | bytes 591360 | tf_op jit(solution)/shard_map/all_gather | solution.py:165
  477.9 1.8 fusion.6
  479.8 3.4 fusion.46
  483.2 4.1 fusion.10
  487.2 2.7 copy.66
  490.5 0.7 copy.68
  491.2 82.9 %reduce-scatter.4.cloned.1.call-done = bf16[80,528]{1,0:T(8,128)(2,1)} async-done(((bf16[1280,528]{1,0:T(8,128)(2,1)}), bf16[80,528]{1,0:T(8,128)(2,1)}) %reduce-scatter.4.cloned.1.call-update) | async-done | bytes 84496
  574.1 1.6 fusion.52
  (87 shorter events, 4.9 us)
Async XLA Ops:
  7.2 69.2 %copy-start.17 = (f32[1280]{0:T(1024)S(1)}, f32[1280]{0:T(1024)}, u32[]{:S(2)}) copy-start(f32[1280]{0:T(1024)} %param.17) | copy-start | bytes 15364
  7.2 67.4 %all-gather.5.cloned.1.call-start = ((), (), s32[]{:S(2)}) async-start(), calls=%async_computation.1 | async-start | bytes 1740800 | tf_op jit(solution)/shard_map/all_gather | solution.py:42
  7.9 131.8 %all-gather.9.cloned.1.call-start = ((), (), s32[]{:S(2)}) async-start(), calls=%async_computation.4 | async-start | bytes 2297856 | tf_op jit(solution)/shard_map/all_gather | solution.py:46
  79.3 1.3 copy-start.5
  79.4 297.0 %all-reduce.3.cloned.1.call-start = ((), (), s32[]{:S(2)}) async-start(), calls=%async_computation.2 | async-start | bytes 3276800 | tf_op jit(solution)/shard_map/psum | solution.py:145
  80.7 1.8 copy-start.16
  160.8 2.6 slice-start.1
  164.6 2.9 slice-start
  164.6 2.9 copy-start
  164.6 3.0 copy-start.15
  170.9 71.5 %copy-start.1 = (bf16[528,320]{1,0:T(8,128)(2,1)S(1)}, bf16[528,320]{1,0:T(8,128)(2,1)}, u32[]{:S(2)}) copy-start(bf16[528,320]{1,0:T(8,128)(2,1)} %get-tuple-element.10) | copy-start | bytes 1013764
  239.2 0.6 copy-start.9
  249.9 6.8 %copy-start.14 = (bf16[40,80]{1,0:T(8,128)(2,1)S(1)}, bf16[40,80]{1,0:T(8,128)(2,1)}, u32[]{:S(2)}) copy-start(bf16[40,80]{1,0:T(8,128)(2,1)} %param.13) | copy-start | bytes 19204
  249.9 38.7 %copy-start.6 = (f32[16,5,4,128]{3,2,1,0:T(4,128)S(1)}, f32[16,5,4,128]{3,2,1,0:T(4,128)}, u32[]{:S(2)}) copy-start(f32[16,5,4,128]{3,2,1,0:T(4,128)} %get-tuple-element.19) | copy-start | bytes 491524
  249.9 38.7 %copy-start.10 = (f32[16,5,4]{2,1,0:T(8,128)S(1)}, f32[16,5,4]{2,1,0:T(8,128)}, u32[]{:S(2)}) copy-start(f32[16,5,4]{2,1,0:T(8,128)} %copy-done.9) | copy-start | bytes 3844
  249.9 39.1 %copy-start.8 = (f32[512,5,4]{0,2,1:T(4,128)S(1)}, f32[512,5,4]{0,2,1:T(4,128)}, u32[]{:S(2)}) copy-start(f32[512,5,4]{0,2,1:T(4,128)} %slice.104) | copy-start | bytes 122884
  256.6 221.3 %all-gather.7.cloned.1.call-start = ((), (), s32[]{:S(2)}) async-start(), calls=%async_computation.3 | async-start | bytes 1740800 | tf_op jit(solution)/shard_map/all_gather | solution.py:156
  293.3 84.8 %copy-start.7 = (bf16[528,80]{0,1:T(8,128)(2,1)S(1)}, bf16[528,80]{0,1:T(8,128)(2,1)}, u32[]{:S(2)}) copy-start(bf16[528,80]{0,1:T(8,128)(2,1)} %param.11) | copy-start | bytes 253444
  378.1 1.2 copy-start.11
  378.1 36.7 %copy-start.12 = (bf16[40,224]{1,0:T(8,128)(2,1)S(1)}, bf16[40,224]{1,0:T(8,128)(2,1)}, u32[]{:S(2)}) copy-start(bf16[40,224]{1,0:T(8,128)(2,1)} %param.15) | copy-start | bytes 53764
  378.1 66.5 %copy-start.13 = (bf16[224,40]{0,1:T(8,128)(2,1)S(1)}, bf16[224,40]{0,1:T(8,128)(2,1)}, u32[]{:S(2)}) copy-start(bf16[224,40]{0,1:T(8,128)(2,1)} %param.16) | copy-start | bytes 53764
  379.2 100.5 %copy-start.18 = (f32[1280]{0:T(1024)S(1)}, f32[1280]{0:T(1024)}, u32[]{:S(2)}) copy-start(f32[1280]{0:T(1024)} %param.18) | copy-start | bytes 15364
  379.3 194.8 %reduce-scatter.4.cloned.1.call-start = ((), (), s32[]{:S(2)}) async-start(), calls=%async_computation.5 | async-start | bytes 1740800
  479.7 3.4 copy-start.4
  487.2 2.7 copy-start.2
  487.2 2.7 copy-start.3
Sparse Core Ops, SparseCore 0:
  11.0 63.4 all-gather.4
  79.5 60.1 all-gather.8
  256.7 119.5 all-reduce.2
  379.8 58.7 all-gather.6
  490.1 83.9 reduce-scatter.3
where the time goes:
time: 583 us; the launch traced here: 582 us
  blocking collectives  305 us (52%)
  waiting for transfers between devices  182 us (31%)
  local copies, waits for them, and re-layouts  33.2 us (6%)
  matrix products  25.9 us (4%)
  other arithmetic  22.6 us (4%)
  between operations  14.2 us (2%)
    unnamed x6, waiting for transfers between devices  83.6 us
    psum x1, blocking collectives, shards(): lax.psum(totals.reshape(row_count, HEADS).astype(jnp.bfloat16), 'wid')  69.2 us
    pmax x1, blocking collectives, shards(): lax.pmax(jnp.maximum(cache_peak, fresh_peak).astype(jnp.bfloat16), 'wid')  67.5 us
    all_gather x1, waiting for transfers between devices, shards(): lax.all_gather(own_cols.astype(jnp.bfloat16), 'wid', axis=1, tiled=True)  55.9 us
    all_gather x1, blocking collectives, shards(): tall_cols = lax.all_gather(w_qkv, 'tok', axis=0, tiled=True)  37.4 us
    all_gather x1, blocking collectives, shards(): lax.all_gather(w_gate, 'tok', axis=0, tiled=True)  35.5 us
    all_gather x1, blocking collectives, shards(): down_full = lax.all_gather(w_down, 'tok', axis=1, tiled=True)  33.2 us
    all_gather x1, blocking collectives, shards(): out_whole = lax.all_gather(w_out, 'tok', axis=0, tiled=True)  31.9 us
  transfers between devices with their start and end apart: 5, of which 4 were waited for; matrix products, arithmetic and copies ran while one was open for 2% of the time, Pallas kernels for 0%

commit v1 on v0

--- a/solution.py
+++ b/solution.py
@@ -142,9 +142,9 @@
         0,
     )
     sums_all, totals_all = (
-        lax.psum(sums.reshape(row_count, query_width).astype(jnp.bfloat16), "wid").astype(
-            jnp.float32
-        ),
+        jnp.sum(
+            lax.all_gather(sums.reshape(row_count, query_width).astype(jnp.bfloat16), "wid"), axis=0
+        ).astype(jnp.float32),
         lax.psum(totals.reshape(row_count, HEADS).astype(jnp.bfloat16), "wid").astype(jnp.float32),
     )
     merged = sums_all.reshape(row_count, HEADS, HEAD_DIM) / totals_all[:, :, None]

time: 583 us -> 629 us (1.079)
  waiting for transfers between devices: 182 us -> 208 us
  other arithmetic: 22.6 us -> 32.3 us
    all_gather x0 -> x1, waiting for transfers between devices: none -> 39.1 us  [shards(): lax.all_gather(sums.reshape(row_count, query_width).astype(jnp.bfloat16),...]
    psum x1 -> x0, waiting for transfers between devices: 12.9 us -> none  [shards(): lax.psum(sums.reshape(row_count, query_width).astype(jnp.bfloat16), 'wid')]
    reduce_sum x0 -> x1, other arithmetic: none -> 12.6 us  [shards(): jnp.sum(lax.all_gather(sums.reshape(row_count, query_width).astype(jnp.bf...]
where the time goes in v1:
time: 629 us; the launch traced here: 628 us
  blocking collectives  308 us (49%)
  waiting for transfers between devices  208 us (33%)
  local copies, waits for them, and re-layouts  39.4 us (6%)
  other arithmetic  32.3 us (5%)
  matrix products  25.7 us (4%)
  between operations  14.2 us (2%)
    unnamed x6, waiting for transfers between devices  83.5 us
    psum x1, blocking collectives, shards(): lax.psum(totals.reshape(row_count, HEADS).astype(jnp.bfloat16), 'wid')  70.1 us
    pmax x1, blocking collectives, shards(): lax.pmax(jnp.maximum(cache_peak, fresh_peak).astype(jnp.bfloat16), 'wid')  67.3 us
    all_gather x1, waiting for transfers between devices, shards(): lax.all_gather(own_cols.astype(jnp.bfloat16), 'wid', axis=1, tiled=True)  56.6 us
    all_gather x1, waiting for transfers between devices, shards(): lax.all_gather(sums.reshape(row_count, query_width).astype(jnp.bfloat16),...  39.1 us
    all_gather x1, blocking collectives, shards(): tall_cols = lax.all_gather(w_qkv, 'tok', axis=0, tiled=True)  37.4 us
    all_gather x1, blocking collectives, shards(): out_whole = lax.all_gather(w_out, 'tok', axis=0, tiled=True)  34.6 us
    all_gather x1, blocking collectives, shards(): down_full = lax.all_gather(w_down, 'tok', axis=1, tiled=True)  33.2 us
  transfers between devices with their start and end apart: 5, of which 4 were waited for; matrix products, arithmetic and copies ran while one was open for 2% of the time, Pallas kernels for 0%

profile of v1, /device:TPU:2, one launch (start us, length us, event | category | flops | bytes accessed | tf_op | source)
XLA Modules:
  0.0 628.1 jit_solution(15950542224097528934)
XLA Ops:
  8.0 37.4 %all_gather.29 = bf16[1280,120]{1,0:T(8,128)(2,1)S(1)} all-gather(bf16[40,120]{1,0:T(8,128)(2,1)} %param.12), channel_id=1, replica_groups=mesh['tok'=32,'wid'=16] {'tok'}, dimensions={0}, use_global_device_ids=true | all-gather | bytes 316800 | tf_op jit(solution)/shard_map/all_gather | solution.py:44
  45.3 29.2 %all-gather.6.cloned.1.call-done = bf16[528,1280]{0,1:T(8,128)(2,1)} async-done(((bf16[528,80]{0,1:T(8,128)(2,1)}), bf16[528,1280]{0,1:T(8,128)(2,1)}) %all-gather.6.cloned.1.call-update) | async-done | bytes 1351696 | tf_op jit(solution)/shard_map/all_gather | solution.py:42
  74.5 1.8 fusion.3
  76.4 3.0 fusion.34
  79.4 1.3 copy-done.8
  80.7 1.2 slice.91
  83.1 56.6 %all-gather.12.cloned.1.call-done = bf16[16,120,528]{1,2,0:T(8,128)(2,1)} async-done(((bf16[1,120,528]{1,2,0:T(8,128)(2,1)}), bf16[16,120,528]{1,2,0:T(8,128)(2,1)}) %all-gather.12.cloned.1.call-update) | async-done | bytes 2027536 | tf_op jit(solution)/shard_map/all_gather | solution.py:46
  139.7 3.5 copy.70
  143.2 3.9 reshape.249
  147.0 1.3 copy-done
  148.3 1.2 fusion.71
  149.6 1.5 slice_convert_fusion
  151.1 2.4 copy.71
  153.5 2.4 subtract_convert_fusion
  156.0 1.2 fusion.26
  157.2 2.6 copy.77
  159.8 2.6 copy.76
  162.8 0.9 multiply_subtract_fusion
  163.8 1.1 fusion.73
  165.1 2.0 fusion.72
  167.1 0.9 dynamic_update_slice.9
  168.0 3.3 bitcast_reduce_fusion
  171.4 67.3 %pmax.7 = bf16[528,5,4]{0,2,1:T(4,128)(2,1)S(1)} all-reduce(bf16[528,5,4]{0,2,1:T(4,128)(2,1)S(1)} %fusion.63), channel_id=1, replica_groups=mesh['tok'=32,'wid'=16] {'wid'}, use_global_device_ids=true, to_apply=%region_4.5 | all-reduce | flops 10560 | bytes 42240 | tf_op jit(solution)/shard_map/pmax | solution.py:104
  238.8 1.2 copy.81
  240.8 2.3 fusion.60
  243.3 3.9 fusion.18
  247.2 1.5 pad_maximum_fusion
  248.7 1.1 fusion.27
  249.8 6.6 %dynamic_update_slice.10 = bf16[528,5,4,64]{0,3,2,1:T(8,128)(2,1)} dynamic-update-slice(bf16[528,5,4,64]{0,3,2,1:T(8,128)(2,1)} %pad_maximum_fusion, bf16[33,5,4,64]{0,3,2,1:T(8,128)(2,1)S(1)} %fusion.27, s32[]{:T(128)S(6)} %select_n.30, s32[]{:T(128)} %constant.13.clone.1, s32[]{:T(128)} %constant.13.clone.1, s32[]{:T(128)} %constant.13.clone.1) | dynamic-update-slice | bytes 168964 | tf_op jit(solution)/shard_map/dynamic_update_slice | solution.py:135
  256.4 2.7 copy.83
  259.2 34.6 %all_gather.32 = bf16[1280,80]{1,0:T(8,128)(2,1)} all-gather(bf16[40,80]{1,0:T(8,128)(2,1)S(1)} %copy-done.17), channel_id=1, replica_groups=mesh['tok'=32,'wid'=16] {'tok'}, dimensions={0}, use_global_device_ids=true | all-gather | bytes 211200 | tf_op jit(solution)/shard_map/all_gather | solution.py:152
  294.2 3.8 fusion.1
  298.7 0.9 dynamic_update_slice.11
  299.6 70.1 %psum.7 = bf16[528,20]{0,1:T(8,128)(2,1)S(1)} all-reduce(bf16[528,20]{0,1:T(8,128)(2,1)S(1)} %convert_element_type.125), channel_id=1, replica_groups=mesh['tok'=32,'wid'=16] {'wid'}, use_global_device_ids=true, to_apply=%region_9.10 | all-reduce | flops 10560 | bytes 42240 | tf_op jit(solution)/shard_map/psum | solution.py:148
  369.9 2.3 copy.85
  372.3 39.1 %all-gather.8.cloned.1.call-done = bf16[16,528,1280]{2,1,0:T(8,128)(2,1)} async-done(((bf16[1,528,1280]{2,1,0:T(8,128)(2,1)}), bf16[16,528,1280]{2,1,0:T(8,128)(2,1)}) %all-gather.8.cloned.1.call-update) | async-done | bytes 21626896 | tf_op jit(solution)/shard_map/all_gather | solution.py:146
  411.4 12.6 %reduce_sum.58 = bf16[528,1280]{1,0:T(8,128)(2,1)} reduce(bf16[16,528,1280]{2,1,0:T(8,128)(2,1)} %all-gather.8.cloned.1.call-done, bf16[]{:T(256)} %constant.15.clone.1), dimensions={0}, to_apply=%region_5.6 | reduce | flops 10137600 | bytes 22978562 | tf_op jit(solution)/shard_map/reduce_sum | solution.py:145
  424.0 2.6 fusion.74
  426.7 32.8 %all_gather.34 = bf16[1280,224]{1,0:T(8,128)(2,1)S(1)} all-gather(bf16[40,224]{1,0:T(8,128)(2,1)S(1)} %copy-done.14), channel_id=1, replica_groups=mesh['tok'=32,'wid'=16] {'tok'}, dimensions={0}, use_global_device_ids=true | all-gather | bytes 591360 | tf_op jit(solution)/shard_map/all_gather | solution.py:159
  459.5 32.5 %all_gather.35 = bf16[1280,224]{1,0:T(8,128)(2,1)} all-gather(bf16[40,224]{1,0:T(8,128)(2,1)S(1)} %copy-done.15), channel_id=1, replica_groups=mesh['tok'=32,'wid'=16] {'tok'}, dimensions={0}, use_global_device_ids=true | all-gather | bytes 591360 | tf_op jit(solution)/shard_map/all_gather | solution.py:160
  492.0 33.2 %all_gather.36 = bf16[224,1280]{0,1:T(8,128)(2,1)} all-gather(bf16[224,40]{0,1:T(8,128)(2,1)S(1)} %copy-done.16), channel_id=1, replica_groups=mesh['tok'=32,'wid'=16] {'tok'}, dimensions={1}, use_global_device_ids=true | all-gather | bytes 591360 | tf_op jit(solution)/shard_map/all_gather | solution.py:165
  525.2 1.8 fusion.6
  527.1 3.3 fusion.47
  530.4 3.2 fusion.9
  533.6 1.7 copy.86
  536.5 0.7 copy.88
  537.2 82.8 %reduce-scatter.4.cloned.1.call-done = bf16[80,528]{1,0:T(8,128)(2,1)} async-done(((bf16[1280,528]{1,0:T(8,128)(2,1)}), bf16[80,528]{1,0:T(8,128)(2,1)}) %reduce-scatter.4.cloned.1.call-update) | async-done | bytes 84496
  620.0 1.6 fusion.53
  (96 shorter events, 6.6 us)
Async XLA Ops:
  7.2 69.2 %copy-start.20 = (f32[1280]{0:T(1024)S(1)}, f32[1280]{0:T(1024)}, u32[]{:S(2)}) copy-start(f32[1280]{0:T(1024)} %param.17) | copy-start | bytes 15364
  7.2 67.4 %all-gather.6.cloned.1.call-start = ((), (), s32[]{:S(2)}) async-start(), calls=%async_computation.1 | async-start | bytes 1740800 | tf_op jit(solution)/shard_map/all_gather | solution.py:42
  7.9 131.8 %all-gather.12.cloned.1.call-start = ((), (), s32[]{:S(2)}) async-start(), calls=%async_computation.4 | async-start | bytes 2297856 | tf_op jit(solution)/shard_map/all_gather | solution.py:46
  79.3 1.3 copy-start.8
  79.4 332.0 %all-gather.8.cloned.1.call-start = ((), (), s32[]{:S(2)}) async-start(), calls=%async_computation.2 | async-start | bytes 22978560 | tf_op jit(solution)/shard_map/all_gather | solution.py:146
  79.4 2.4 copy-start.19
  147.0 1.3 copy-start
  159.8 2.6 copy-start.3
  162.4 1.4 slice-start.1
  165.1 2.9 slice-start
  165.1 2.9 copy-start.1
  165.1 3.0 copy-start.18
  171.4 72.0 %slice-start.2 = ((bf16[17,128,320]{1,2,0:T(8,128)(2,1)}), bf16[1,128,320]{1,2,0:T(8,128)(2,1)S(1)}, s32[]{:S(2)}) async-start(bf16[17,128,320]{1,2,0:T(8,128)(2,1)} %param.21), calls=%async_computation.8 | async-start | bytes 163840 | tf_op jit(solution)/shard_map/slice | solution.py:117
  247.2 1.5 copy-start.12
  256.4 2.7 copy-start.17
  256.4 37.3 %copy-start.9 = (f32[16,5,4,128]{3,2,1,0:T(4,128)S(1)}, f32[16,5,4,128]{3,2,1,0:T(4,128)}, u32[]{:S(2)}) copy-start(f32[16,5,4,128]{3,2,1,0:T(4,128)} %get-tuple-element.21) | copy-start | bytes 491524
  259.1 266.1 %all-gather.10.cloned.1.call-start = ((), (), s32[]{:S(2)}) async-start(), calls=%async_computation.3 | async-start | bytes 1740800 | tf_op jit(solution)/shard_map/all_gather | solution.py:156
  294.2 3.8 copy-start.13
  372.3 51.7 %copy-start.4 = (f32[528,1280]{1,0:T(8,128)S(1)}, f32[528,1280]{1,0:T(8,128)}, u32[]{:S(2)}) copy-start(f32[528,1280]{1,0:T(8,128)} %copy.85) | copy-start | bytes 8110084
  372.3 51.7 %copy-start.10 = (bf16[1280,80]{1,0:T(8,128)(2,1)S(1)}, bf16[1280,80]{1,0:T(8,128)(2,1)}, u32[]{:S(2)}) copy-start(bf16[1280,80]{1,0:T(8,128)(2,1)} %all_gather.32) | copy-start | bytes 614404
  372.3 51.7 %copy-start.11 = (bf16[528,80]{0,1:T(8,128)(2,1)S(1)}, bf16[528,80]{0,1:T(8,128)(2,1)}, u32[]{:S(2)}) copy-start(bf16[528,80]{0,1:T(8,128)(2,1)} %param.11) | copy-start | bytes 253444
  424.0 2.7 copy-start.14
  424.0 35.5 %copy-start.15 = (bf16[40,224]{1,0:T(8,128)(2,1)S(1)}, bf16[40,224]{1,0:T(8,128)(2,1)}, u32[]{:S(2)}) copy-start(bf16[40,224]{1,0:T(8,128)(2,1)} %param.15) | copy-start | bytes 53764
  424.0 68.0 %copy-start.16 = (bf16[224,40]{0,1:T(8,128)(2,1)S(1)}, bf16[224,40]{0,1:T(8,128)(2,1)}, u32[]{:S(2)}) copy-start(bf16[224,40]{0,1:T(8,128)(2,1)} %param.16) | copy-start | bytes 53764
  426.6 100.5 %copy-start.21 = (f32[1280]{0:T(1024)S(1)}, f32[1280]{0:T(1024)}, u32[]{:S(2)}) copy-start(f32[1280]{0:T(1024)} %param.18) | copy-start | bytes 15364
  426.6 193.4 %reduce-scatter.4.cloned.1.call-start = ((), (), s32[]{:S(2)}) async-start(), calls=%async_computation.5 | async-start | bytes 1740800
  527.1 3.3 copy-start.7
  533.5 1.7 copy-start.5
  533.5 1.7 copy-start.6
  535.3 1.0 copy-start.2
Sparse Core Ops, SparseCore 0:
  11.0 63.4 all-gather.5
  79.5 60.1 all-gather.11
  259.3 152.0 all-gather.7
  426.7 59.4 all-gather.9
  535.4 84.5 reduce-scatter.3
